TPU v7x, 512 devices: a whole 4x4x16 slice. The times are simulated.
512 devices in a mesh: rep: 64 (over z_hi, x, y, core), fsdp: 8 (over z_lo).
Axes of the slice: x: 4, y: 4, z: 16 (z_hi: 2, z_lo: 8; z = z_hi * 8 + z_lo), core: 2. Of those that a mesh axis runs over, the one named last changes fastest.
Arguments:
- tokens: bfloat16 [49152, 4096], P(('rep', 'fsdp')), may hold values from -6 to 6
- norm_gain: float32 [4096], replicated, may hold values from 0.1 to 1.9
- target: bfloat16 [49152, 2, 1024], P('rep', None, 'fsdp'), may hold values from -6 to 6
- master: float32 [2, 4096, 1024], P(None, 'rep', 'fsdp'), may hold values from -0.09375 to 0.09375
- momentum: float32 [2, 4096, 1024], P(None, 'rep', 'fsdp'), may hold values from -4 to 4
Outputs:
- new_master: float32 [2, 4096, 1024], P(None, 'rep', 'fsdp')
- new_momentum: float32 [2, 4096, 1024], P(None, 'rep', 'fsdp')
All inputs are finite; a program needn't handle non-finite values.
Results may differ from a plain program's by a relative error of at most 0.00067.
Values may be sent and summed in bfloat16 or wider, within the bound.
A program may use at most 64 MiB of HBM per device.

v0:
```python
import jax
import jax.numpy as jnp
from jax import lax
from jax.sharding import PartitionSpec as P

inner_rate = 0.02
outer_rate = 0.7
decay_rate = 0.9
norm_eps = 1e-05


def body(tokens, norm_gain, target, master, momentum):
    values = tokens.astype(jnp.float32)
    scale = lax.rsqrt(jnp.mean(values * values, axis=-1, keepdims=True) + norm_eps)
    normed = (values * scale * norm_gain).astype(jnp.bfloat16)
    weights = lax.all_gather(master.astype(jnp.bfloat16), "rep", axis=1, tiled=True)
    piece = lax.all_gather(normed, "fsdp", axis=0, tiled=True)
    predicted = jnp.einsum("rd,sdc->rsc", piece, weights, preferred_element_type=jnp.float32)
    goal = target.astype(jnp.float32)
    error = (predicted - goal).astype(jnp.bfloat16)
    grads = jnp.einsum("rd,rsc->sdc", piece, error, preferred_element_type=jnp.float32)
    summed = lax.psum_scatter(grads, "rep", scatter_dimension=1, tiled=True)
    delta = summed * (inner_rate / lax.axis_size("rep"))
    new_momentum = decay_rate * momentum + delta
    new_master = master - outer_rate * (delta + decay_rate * new_momentum)
    return (new_master, new_momentum)


def solution(mesh):
    in_specs = (
        P(("rep", "fsdp"), None),
        P(),
        P("rep", None, "fsdp"),
        P(None, "rep", "fsdp"),
        P(None, "rep", "fsdp"),
    )
    out_specs = (P(None, "rep", "fsdp"), P(None, "rep", "fsdp"))
    return jax.shard_map(body, mesh=mesh, in_specs=in_specs, out_specs=out_specs, check_vma=False)
```

profile of v0, /device:TPU:1, one launch (start us, length us, event | category | flops | bytes accessed | tf_op | source)
XLA Modules:
  0.0 1381.8 jit_solution(12803080520559578777)
XLA Ops:
  7.2 0.0 all-gather.5.cloned.1.call-start
  7.2 1.5 convert_element_type.17
  8.7 0.0 all-gather.5.cloned.1.call-update
  8.7 0.0 all-gather.3.cloned.1.call-start
  8.7 1.4 fusion.7
  10.1 2.3 fusion.9
  12.4 0.0 all-gather.3.cloned.1.call-update
  12.5 0.0 all-reduce.3.cloned.1.call-start
  12.5 120.5 %all-gather.5.cloned.1.call-done = bf16[2,4096,128]{2,1,0:T(8,128)(2,1)} async-done(((bf16[2,64,128]{2,1,0:T(8,128)(2,1)}), bf16[2,4096,128]{2,1,0:T(8,128)(2,1)}) %all-gather.5.cloned.1.call-update) | async-done | bytes 2097168 | tf_op jit(solution)/shard_map/all_gather | solution.py:16
  133.0 133.6 %all-gather.3.cloned.1.call-done = bf16[768,4096]{1,0:T(8,128)(2,1)} async-done(((bf16[96,4096]{1,0:T(8,128)(2,1)}), bf16[768,4096]{1,0:T(8,128)(2,1)}) %all-gather.3.cloned.1.call-update) | async-done | bytes 6291472 | tf_op jit(solution)/shard_map/all_gather | solution.py:17
  266.6 14.0 %fusion.4 = f32[2,4096,128]{1,2,0:T(8,128)} fusion(bf16[768,4096]{1,0:T(8,128)(2,1)} %all-gather.3.cloned.1.call-done, bf16[2,4096,128]{2,1,0:T(8,128)(2,1)} %all-gather.5.cloned.1.call-done, bf16[768,2,128]{2,1,0:T(2,128)(2,1)} %param.7), kind=kOutput, calls=%fused_computation.4 | convolution fusion | flops 3221815296 | bytes 12976128 | tf_op jit(solution)/shard_map/rd,rsc->sdc/dot_general | solution.py:21
  280.6 7.2 copy.20
  287.8 0.0 copy-start
  287.8 0.0 copy-start.1
  287.8 0.0 all-reduce.3.cloned.1.call-update
  287.8 1.3 dynamic-slice
  289.8 1084.0 %all-reduce.3.cloned.1.call-done = f32[2,4096,128]{2,0,1:T(2,128)} async-done(((f32[2,4096,128]{2,0,1:T(2,128)}), f32[2,4096,128]{2,0,1:T(2,128)}) %all-reduce.3.cloned.1.call-update) | async-done | bytes 4194320
  1373.8 0.8 constant_dynamic-slice_fusion
  1374.6 0.0 copy-done
  1374.6 0.0 copy-done.1
  1374.6 0.7 multiply_subtract_fusion
  (1 shorter events, 0.0 us)
Async XLA Ops:
  7.2 125.8 %all-gather.5.cloned.1.call-start = ((), (), s32[]{:S(2)}) async-start(), calls=%async_computation.1 | async-start | bytes 2129920 | tf_op jit(solution)/shard_map/all_gather | solution.py:16
  8.7 257.9 %all-gather.3.cloned.1.call-start = ((), (), s32[]{:S(2)}) async-start(), calls=%async_computation | async-start | bytes 7077888 | tf_op jit(solution)/shard_map/all_gather | solution.py:17
  12.5 1361.3 %all-reduce.3.cloned.1.call-start = ((), (), s32[]{:S(2)}) async-start(), calls=%async_computation.2 | async-start | bytes 8388608
  287.8 1086.8 %copy-start = (f32[2,64,128]{2,1,0:T(8,128)S(1)}, f32[2,64,128]{2,1,0:T(8,128)}, u32[]{:S(2)}) copy-start(f32[2,64,128]{2,1,0:T(8,128)} %param.8) | copy-start | bytes 196612
  287.8 1086.8 %copy-start.1 = (f32[2,64,128]{2,1,0:T(8,128)S(1)}, f32[2,64,128]{2,1,0:T(8,128)}, u32[]{:S(2)}) copy-start(f32[2,64,128]{2,1,0:T(8,128)} %param.9) | copy-start | bytes 196612
Sparse Core Ops, SparseCore 0:
  13.1 119.8 all-gather.4
  135.0 131.4 all-gather.2
  287.9 1085.7 all-reduce.2
where the time goes:
time: 1380 us
  waiting for transfers between devices  1340 us (97%)
  between operations  14.4 us (1%)
  matrix products  14 us (1%)
    unnamed x4, waiting for transfers between devices  1080 us
    all_gather x1, waiting for transfers between devices, body(): piece = lax.all_gather(normed, 'fsdp', axis=0, tiled=True)  134 us
    all_gather x1, waiting for transfers between devices, body(): lax.all_gather(master.astype(jnp.bfloat16), 'rep', axis=1, tiled=True)  120 us
  transfers between devices with their start and end apart: 3, of which 3 were waited for; matrix products, arithmetic and copies ran while one was open for 0% of the time, Pallas kernels for 0%

commit v1 on v0

v1 whole, which is shorter than its diff:
```python
import jax
import jax.numpy as jnp
from jax import lax
from jax.experimental import pallas as pl
from jax.experimental.pallas import tpu as pltpu
from jax.sharding import PartitionSpec as P

inner_rate = 0.02
outer_rate = 0.7
decay_rate = 0.9
norm_eps = 1e-05

MESH = pl.DeviceIdType.MESH
NX = 4
NY = 4
LEVELS = 16
HALF = 8
CLASSES = 4
TOK = 96
CHUNKS = 3
ROWS = TOK // CHUNKS
D = 4096
f32 = jnp.float32
bf16 = jnp.bfloat16


def encode(v):
    return (v * jnp.abs(v) * (v * v)).astype(bf16)


def decode(w):
    w = w.astype(f32)
    r = lax.rsqrt(lax.rsqrt(jnp.maximum(jnp.abs(w), 1.2e-38)))
    return jnp.where(w < 0, -r, r)


def kernel(
    tok_ref, gain_ref, tgt_ref, master_ref, mom_ref,
    out_master, out_mom,
    xall, wsh, wg, tg, et, gf, gb, r1a, r1b, af, bfull, a1, b1, r2a, r2b, g3, r3,
    w_send, w_recv, ag1_send, ag1_recv, ag2_send, ag2_recv,
    x1_send, x1_recv, x3_send, x3_recv, x2_send, x2_recv, d_send, d_recv,
    t_send, t_recv, g1_send, g1_recv, g2_send, g2_recv, g3_send, g3_recv,
):
    rep = lax.axis_index("rep")
    lev = lax.axis_index("fsdp")
    core = lax.rem(rep, 2)
    y = lax.rem(rep // 2, NY)
    x = lax.rem(rep // (2 * NY), NX)
    half = rep // (2 * NY * NX)
    z = half * HALF + lev
    cls = lax.rem(lev, CLASSES)
    kt = lev // CLASSES
    col = cls + CLASSES * core
    fdir = 2 * core - 1
    sg = -fdir

    def at(h, xx, yy, c, level):
        return (((h * NX + xx) * NY + yy) * 2 + c, level)

    def at_z(zz, c):
        zz = lax.rem(zz + LEVELS, LEVELS)
        return at(zz // HALF, x, y, c, lax.rem(zz, HALF))

    def rdma(src, dst, ss, rs, dev):
        return pltpu.make_async_remote_copy(
            src_ref=src, dst_ref=dst, send_sem=ss, recv_sem=rs, device_id=dev, device_id_type=MESH
        )

    xpeer = [at(half, lax.rem(x + j, NX), y, core, lev) for j in (1, 2, 3)]
    ypeer = [at(half, x, lax.rem(y + j, NY), core, lev) for j in (1, 2, 3)]
    up = at_z(z + fdir, core)
    down = at_z(z - fdir, core)
    twin = at_z(z, 1 - core)

    barrier = pltpu.get_barrier_semaphore()

    def hello(dev):
        pl.semaphore_signal(barrier, inc=1, device_id=dev, device_id_type=MESH)

    for dev in xpeer + ypeer + [up, down, twin]:
        hello(dev)
    native = lax.rem(kt + core, 2) == 0
    for m in range(4):
        dz = cls + CLASSES * m

        @pl.when(jnp.logical_not(jnp.logical_and(dz == z, native)))
        def _():
            hello(at_z(dz, kt))

        h2, c2 = m // 2, m % 2

        @pl.when(jnp.logical_not(jnp.logical_and(native, jnp.logical_and(h2 == half, c2 == core))))
        def _():
            hello(at(h2, x, y, c2, col))

    gain = gain_ref[...]
    for c in range(CHUNKS):
        v = tok_ref[pl.ds(c * ROWS, ROWS), :].astype(f32)
        scale = lax.rsqrt(jnp.mean(v * v, axis=-1, keepdims=True) + norm_eps)
        xall[pl.ds(c * ROWS, ROWS), :] = (v * scale * gain).astype(bf16)
    wsh[...] = master_ref[...].astype(bf16)

    pl.semaphore_wait(barrier, 9 + 8 - 2 * (1 - lax.rem(kt + core, 2)))

    sidx = half * 2 + core
    wdst = wg.at[:, half, x, y, pl.ds(pl.multiple_of(core * 64, 64), 64), :]

    def w_copy(m):
        return rdma(wsh, wdst, w_send.at[m], w_recv.at[sidx], at_z(cls + CLASSES * m, kt))

    def w_local():
        return pltpu.make_async_copy(wsh, wdst, w_recv.at[sidx])

    for m in range(4):
        mine = jnp.logical_and(cls + CLASSES * m == z, native)

        @pl.when(mine)
        def _():
            w_local().start()

        @pl.when(jnp.logical_not(mine))
        def _():
            w_copy(m).start()

    def slot(s, c, other=False):
        return xall.at[pl.ds((384 if other else 0) + s * TOK + c * ROWS, ROWS), :]

    def x1(c):
        return rdma(slot(0, c), slot(1, c), x1_send.at[c], x1_recv.at[c], up)

    def x3(c):
        return rdma(slot(0, c), slot(3, c), x3_send.at[c], x3_recv.at[c], down)

    def x2(c):
        return rdma(slot(1, c), slot(2, c), x2_send.at[c], x2_recv.at[c], up)

    def to_twin(s, c):
        i = s * CHUNKS + c
        return rdma(slot(s, c), slot(s, c, True), d_send.at[i], d_recv.at[i], twin)

    for c in range(CHUNKS):
        x1(c).start()
        x3(c).start()
    for c in range(CHUNKS):
        to_twin(0, c).start()

    def t_parts(i):
        s = lax.rem(sg * (i - lev) + 8, 4)
        m = s - 4 * (s // 3)
        zt = lax.rem(half * HALF + i - sg * m + LEVELS, LEVELS)
        row = pl.multiple_of((lax.rem(kt + core, 2) * 4 + s) * TOK, TOK)
        idx = lax.rem(kt + core, 2) * 4 + s
        self_ = jnp.logical_and(zt == z, native)
        return tgt_ref.at[:, pl.ds(i * TOK, TOK), :], tg.at[:, pl.ds(row, TOK), :], idx, zt, self_

    for i in range(8):
        src, dst, idx, zt, self_ = t_parts(i)

        @pl.when(self_)
        def _():
            pltpu.make_async_copy(src, dst, t_recv.at[idx]).start()

        @pl.when(jnp.logical_not(self_))
        def _():
            rdma(src, dst, t_send.at[i], t_recv.at[idx], at_z(zt, kt)).start()

    for i in range(4):
        wd = wg.at[:, i // 2, x, y, pl.ds((i % 2) * 64, 64), :]
        rdma(wsh, wd, w_send.at[0], w_recv.at[i], twin).wait_recv()

    def ag1(b, j):
        r = wg.at[b, :, x, y]
        return rdma(r, r, ag1_send.at[b * 3 + j], ag1_recv.at[b * 3 + j], (xpeer if b == 0 else ypeer)[j])

    def ag2(b, j):
        r = wg.at[0, :, :, y] if b == 0 else wg.at[1, :, x]
        return rdma(r, r, ag2_send.at[b * 3 + j], ag2_recv.at[b * 3 + j], (ypeer if b == 0 else xpeer)[j])

    pairs = [(b, j) for j in range(3) for b in range(2)]
    for b, j in pairs:
        ag1(b, j).start()
    for b, j in pairs:
        ag1(b, j).wait_recv()
    for b, j in pairs:
        ag2(b, j).start()

    for c in range(CHUNKS):
        x1(c).wait_recv()
        x2(c).start()
        to_twin(1, c).start()
        x3(c).wait_recv()
        to_twin(3, c).start()
    for c in range(CHUNKS):
        x2(c).wait_recv()
        to_twin(2, c).start()

    for b, j in pairs:
        ag2(b, j).wait_recv()
    for s in (0, 1, 3, 2):
        for c in range(CHUNKS):
            to_twin(s, c).wait_recv()
    for i in range(8):
        dst = tg.at[:, pl.ds(i * TOK, TOK), :]
        rdma(dst, dst, t_send.at[0], t_recv.at[i], twin).wait_recv()

    def forward(i, _):
        r = pl.ds(pl.multiple_of(i * 256, 256), 256)
        w = jnp.concatenate([wg[0].reshape(D, 128), wg[1].reshape(D, 128)], axis=1)
        p = jnp.dot(xall[r, :], w, preferred_element_type=f32)
        goal = jnp.concatenate([tg[0, r, :], tg[1, r, :]], axis=1).astype(f32)
        et[i] = jnp.transpose(p - goal).astype(bf16)
        return 0

    lax.fori_loop(0, 3, forward, 0)

    def backward(t, _):
        cols = pl.ds(pl.multiple_of(t * 512, 512), 512)
        e = jnp.concatenate([et[0], et[1], et[2]], axis=1)
        g = jnp.dot(e, xall[:, cols], preferred_element_type=f32)
        for b in range(2):
            for yy in range(NY):
                piece = g[b * 128:(b + 1) * 128, yy * 128:(yy + 1) * 128]
                gf[b, t // NX, lax.rem(t, NX), yy] = piece
                gb[b, t // NX, lax.rem(t, NX), yy] = encode(piece)
        return 0

    lax.fori_loop(0, 8, backward, 0)

    def g1(b, j):
        if b == 0:
            src, dst = gb.at[0, :, lax.rem(x + j + 1, NX)], r1a.at[j]
        else:
            src, dst = gb.at[1, :, :, lax.rem(y + j + 1, NY)], r1b.at[j]
        return rdma(src, dst, g1_send.at[b * 3 + j], g1_recv.at[b * 3 + j], (xpeer if b == 0 else ypeer)[j])

    for b, j in pairs:
        g1(b, j).start()
    for b, j in pairs:
        g1(b, j).wait_recv()

    def sum1(t, _):
        h, i = t // 4, lax.rem(t, 4)
        va = gf[0, h, x, i] + decode(r1a[0, h, i]) + decode(r1a[1, h, i]) + decode(r1a[2, h, i])
        vb = gf[1, h, i, y] + decode(r1b[0, h, i]) + decode(r1b[1, h, i]) + decode(r1b[2, h, i])
        af[h, i] = va
        bfull[h, i] = vb
        a1[h, i] = encode(va)
        b1[h, i] = encode(vb)
        return 0

    lax.fori_loop(0, 8, sum1, 0)

    def g2(b, j):
        if b == 0:
            src, dst = a1.at[:, lax.rem(y + j + 1, NY)], r2a.at[j]
        else:
            src, dst = b1.at[:, lax.rem(x + j + 1, NX)], r2b.at[j]
        return rdma(src, dst, g2_send.at[b * 3 + j], g2_recv.at[b * 3 + j], (ypeer if b == 0 else xpeer)[j])

    for b, j in pairs:
        g2(b, j).start()
    for b, j in pairs:
        g2(b, j).wait_recv()
    for h in range(2):
        va = af[h, y] + decode(r2a[0, h]) + decode(r2a[1, h]) + decode(r2a[2, h])
        vb = bfull[h, x] + decode(r2b[0, h]) + decode(r2b[1, h]) + decode(r2b[2, h])
        g3[h, 0] = encode(jnp.transpose(va))
        g3[h, 1] = encode(jnp.transpose(vb))

    m_own = z // CLASSES

    def g3_parts(i):
        h2, c2 = i // 2, i % 2
        src = g3.at[h2, :, pl.ds(c2 * 64, 64), :]
        self_ = jnp.logical_and(native, jnp.logical_and(half == h2, core == c2))
        return src, r3.at[m_own], at(h2, x, y, c2, col), self_

    for i in range(4):
        src, dst, dev, self_ = g3_parts(i)

        @pl.when(self_)
        def _():
            pltpu.make_async_copy(src, dst, g3_recv.at[m_own]).start()

        @pl.when(jnp.logical_not(self_))
        def _():
            rdma(src, dst, g3_send.at[i], g3_recv.at[m_own], dev).start()

    for i in range(4):
        rdma(r3.at[i], r3.at[i], g3_send.at[0], g3_recv.at[i], twin).wait_recv()

    total = decode(r3[0]) + decode(r3[1]) + decode(r3[2]) + decode(r3[3])
    delta = total * (inner_rate / 64)
    new_mom = decay_rate * mom_ref[...] + delta
    out_mom[...] = new_mom
    out_master[...] = master_ref[...] - outer_rate * (delta + decay_rate * new_mom)

    for m in range(4):
        @pl.when(jnp.logical_not(jnp.logical_and(cls + CLASSES * m == z, native)))
        def _():
            w_copy(m).wait_send()
    for c in range(CHUNKS):
        x1(c).wait_send()
        x2(c).wait_send()
        x3(c).wait_send()
        for s in range(4):
            to_twin(s, c).wait_send()
    for i in range(8):
        src, dst, idx, zt, self_ = t_parts(i)

        @pl.when(jnp.logical_not(self_))
        def _():
            rdma(src, dst, t_send.at[i], t_recv.at[idx], at_z(zt, kt)).wait_send()
    for b, j in pairs:
        ag1(b, j).wait_send()
        ag2(b, j).wait_send()
        g1(b, j).wait_send()
        g2(b, j).wait_send()
    for i in range(4):
        src, dst, dev, self_ = g3_parts(i)

        @pl.when(jnp.logical_not(self_))
        def _():
            rdma(src, dst, g3_send.at[i], g3_recv.at[m_own], dev).wait_send()


def body(tokens, norm_gain, target, master, momentum):
    goal = jnp.transpose(target, (1, 0, 2))
    vm = pl.BlockSpec(memory_space=pltpu.VMEM)
    dma = pltpu.SemaphoreType.DMA
    shard = jax.ShapeDtypeStruct(master.shape, f32)
    V = pltpu.VMEM
    scratch = [
        V((768, D), bf16),
        V((2, 64, 128), bf16),
        V((2, 2, NX, NY, 128, 128), bf16),
        V((2, 768, 128), bf16),
        V((3, 256, 256), bf16),
        V((2, 2, NX, NY, 128, 128), f32),
        V((2, 2, NX, NY, 128, 128), bf16),
        V((3, 2, NY, 128, 128), bf16),
        V((3, 2, NX, 128, 128), bf16),
        V((2, NY, 128, 128), f32),
        V((2, NX, 128, 128), f32),
        V((2, NY, 128, 128), bf16),
        V((2, NX, 128, 128), bf16),
        V((3, 2, 128, 128), bf16),
        V((3, 2, 128, 128), bf16),
        V((2, 2, 128, 128), bf16),
        V((4, 2, 64, 128), bf16),
        dma((4,)), dma((4,)), dma((6,)), dma((6,)), dma((6,)), dma((6,)),
        dma((CHUNKS,)), dma((CHUNKS,)), dma((CHUNKS,)), dma((CHUNKS,)), dma((CHUNKS,)), dma((CHUNKS,)),
        dma((4 * CHUNKS,)), dma((4 * CHUNKS,)),
        dma((8,)), dma((8,)), dma((6,)), dma((6,)), dma((6,)), dma((6,)), dma((4,)), dma((4,)),
    ]
    return pl.pallas_call(
        kernel,
        out_shape=(shard, shard),
        in_specs=[vm] * 5,
        out_specs=(vm, vm),
        scratch_shapes=scratch,
        compiler_params=pltpu.CompilerParams(
            collective_id=0, has_side_effects=True, vmem_limit_bytes=48 * 1024 * 1024
        ),
        cost_estimate=pl.CostEstimate(flops=3_300_000_000, bytes_accessed=2_000_000, transcendentals=0),
    )(tokens, norm_gain.reshape(1, D), goal, master, momentum)


def solution(mesh):
    in_specs = (
        P(("rep", "fsdp"), None),
        P(),
        P("rep", None, "fsdp"),
        P(None, "rep", "fsdp"),
        P(None, "rep", "fsdp"),
    )
    out_specs = (P(None, "rep", "fsdp"), P(None, "rep", "fsdp"))
    return jax.shard_map(body, mesh=mesh, in_specs=in_specs, out_specs=out_specs, check_vma=False)
```

time: 1380 us -> 106 us (0.08)
  waiting for transfers between devices: 1340 us -> 0 us
  Pallas kernels: 0 us -> 101 us
  matrix products: 14 us -> 0 us
    unnamed x4 -> x0, waiting for transfers between devices: 1080 us -> none
    all_gather x2 -> x0, waiting for transfers between devices: 254 us -> none  [the longest x1 134 us: body(): piece = lax.all_gather(normed, 'fsdp', axis=0, tiled=True)]
    pallas_call x0 -> x1, Pallas kernels: none -> 101 us  [body(): pl.pallas_call(kernel, out_shape=(shard, shard), in_specs=[vm] * 5, out_s...]
    dot_general x1 -> x0, matrix products: 14 us -> none  [body(): jnp.einsum('rd,rsc->sdc', piece, error, preferred_element_type=jnp.float32)]
  transfers between devices with their start and end apart: 3 -> 0, of which waited for: 3 -> 0; matrix products, arithmetic and copies ran while one was open for 0% -> 0% of each run, Pallas kernels for 0% -> 0%
where the time goes in v1:
time: 106 us
  Pallas kernels  101 us (95%)
  local copies, waits for them, and re-layouts  4.9 us (5%)
    pallas_call x1, Pallas kernels, body(): pl.pallas_call(kernel, out_shape=(shard, shard), in_specs=[vm] * 5, out_s...  101 us
    unnamed x11, local copies, waits for them, and re-layouts  4.9 us

profile of v1, /device:TPU:1, one launch (start us, length us, event | category | flops | bytes accessed | tf_op | source)
XLA Modules:
  0.0 106.2 jit_solution(17746675451323969357)
XLA Ops:
  0.6 0.0 copy-start
  0.6 1.1 %copy.9 = bf16[768,2,128]{2,0,1:T(8,128)(2,1)S(1)} copy(bf16[768,2,128]{2,1,0:T(2,128)(2,1)} %param.7) | data formatting | bytes 786432 | tf_op args[2]
  1.8 0.1 copy-done
  1.9 0.0 copy-start.1
  1.9 0.8 copy-done.1
  2.7 0.0 copy-start.2
  2.7 0.8 copy-done.2
  3.6 0.0 copy-start.3
  3.6 0.7 copy-done.3
  4.3 100.6 %shard_map.68 = (f32[2,64,128]{2,1,0:T(8,128)S(1)}, f32[2,64,128]{2,1,0:T(8,128)S(1)}) custom-call(bf16[96,4096]{1,0:T(8,128)(2,1)S(1)} %copy-done, f32[1,4096]{1,0:T(1,128)S(1)} %bitcast.5, bf16[2,768,128]{2,1,0:T(8,128)(2,1)S(1)} %bitcast.4, f32[2,64,128]{2,1,0:T(8,128)S(1)} %copy-done.1, f32[2,64,128]{2,1,0:T(8,128)S(1)} %copy-done.2), custom_call_target="tpu_custom_call" | custom-call | flops 3300000000 | bytes 2000000 | tf_op jit(solution)/shard_map/pallas_call | solution.py:357
  104.9 0.6 copy.12
  105.5 0.6 copy.13
Async XLA Ops:
  0.6 1.3 %copy-start = (bf16[96,4096]{1,0:T(8,128)(2,1)S(1)}, bf16[96,4096]{1,0:T(8,128)(2,1)}, u32[]{:S(2)}) copy-start(bf16[96,4096]{1,0:T(8,128)(2,1)} %tok_ref.1) | copy-start | bytes 2359300
  1.9 0.8 copy-start.1
  2.7 0.8 copy-start.2
  3.6 0.7 copy-start.3

commit v2 on v1

v2 whole, which is shorter than its diff:
```python
import jax
import jax.numpy as jnp
from jax import lax
from jax.experimental import pallas as pl
from jax.experimental.pallas import tpu as pltpu
from jax.sharding import PartitionSpec as P

inner_rate = 0.02
outer_rate = 0.7
decay_rate = 0.9
norm_eps = 1e-05

MESH = pl.DeviceIdType.MESH
NX = 4
NY = 4
LEVELS = 16
HALF = 8
CLASSES = 4
TOK = 96
CHUNKS = 3
ROWS = TOK // CHUNKS
D = 4096
f32 = jnp.float32
bf16 = jnp.bfloat16


def encode(v):
    return (v * jnp.abs(v) * (v * v)).astype(bf16)


def decode(w):
    w = w.astype(f32)
    r = lax.rsqrt(lax.rsqrt(jnp.maximum(jnp.abs(w), 1.2e-38)))
    return jnp.where(w < 0, -r, r)


def kernel(
    tok_ref, gain_ref, goal_ref, master_ref,
    out_ref,
    xin, gain, mst, xall, wsh, wg, tg, pred, et, own, gb, r1, mid, a1, r2, g3, r3,
    in_sem, w_send, w_recv, ag1_send, ag1_recv, ag2_send, ag2_recv,
    x1_send, x1_recv, x3_send, x3_recv, x2_send, x2_recv, d_send, d_recv,
    t_send, t_recv, g1_send, g1_recv, g2_send, g2_recv, g3_send, g3_recv,
):
    loads = [
        pltpu.make_async_copy(src, dst, in_sem.at[i])
        for i, (src, dst) in enumerate(((tok_ref, xin), (gain_ref, gain), (master_ref, mst)))
    ]
    for load in loads:
        load.start()

    rep = lax.axis_index("rep")
    lev = lax.axis_index("fsdp")
    core = lax.rem(rep, 2)
    y = lax.rem(rep // 2, NY)
    x = lax.rem(rep // (2 * NY), NX)
    half = rep // (2 * NY * NX)
    z = half * HALF + lev
    cls = lax.rem(lev, CLASSES)
    kt = lev // CLASSES
    col = cls + CLASSES * core
    fdir = 2 * core - 1
    sg = -fdir
    foreign = lax.rem(kt + core, 2)
    native = foreign == 0

    def at(h, xx, yy, c, level):
        return (((h * NX + xx) * NY + yy) * 2 + c, level)

    def at_z(zz, c):
        zz = lax.rem(zz + LEVELS, LEVELS)
        return at(zz // HALF, x, y, c, lax.rem(zz, HALF))

    def rdma(src, dst, ss, rs, dev):
        return pltpu.make_async_remote_copy(
            src_ref=src, dst_ref=dst, send_sem=ss, recv_sem=rs, device_id=dev, device_id_type=MESH
        )

    xpeer = [at(half, lax.rem(x + j, NX), y, core, lev) for j in (1, 2, 3)]
    ypeer = [at(half, x, lax.rem(y + j, NY), core, lev) for j in (1, 2, 3)]
    up = at_z(z + fdir, core)
    down = at_z(z - fdir, core)
    twin = at_z(z, 1 - core)

    barrier = pltpu.get_barrier_semaphore()

    def hello(dev):
        pl.semaphore_signal(barrier, inc=1, device_id=dev, device_id_type=MESH)

    for dev in xpeer + ypeer + [up, down, twin]:
        hello(dev)
    for m in range(4):
        dz = cls + CLASSES * m

        @pl.when(jnp.logical_not(jnp.logical_and(dz == z, native)))
        def _():
            hello(at_z(dz, kt))

        h2, c2 = m // 2, m % 2

        @pl.when(jnp.logical_not(jnp.logical_and(native, jnp.logical_and(h2 == half, c2 == core))))
        def _():
            hello(at(h2, x, y, c2, col))

    for load in loads:
        load.wait()
    wsh[...] = mst[...].astype(bf16)
    for c in range(CHUNKS):
        v = xin[pl.ds(c * ROWS, ROWS), :].astype(f32)
        scale = lax.rsqrt(jnp.mean(v * v, axis=-1, keepdims=True) + norm_eps)
        xall[pl.ds(c * ROWS, ROWS), :] = (v * scale * gain[...]).astype(bf16)

    pl.semaphore_wait(barrier, 9 + 8 - 2 * (1 - foreign))

    sidx = half * 2 + core
    wdst = wg.at[:, half, x, y, pl.ds(pl.multiple_of(core * 64, 64), 64), :]

    def w_copy(m):
        return rdma(wsh, wdst, w_send.at[m], w_recv.at[sidx], at_z(cls + CLASSES * m, kt))

    for m in range(4):
        mine = jnp.logical_and(cls + CLASSES * m == z, native)

        @pl.when(mine)
        def _():
            pltpu.make_async_copy(wsh, wdst, w_recv.at[sidx]).start()

        @pl.when(jnp.logical_not(mine))
        def _():
            w_copy(m).start()

    base = ((0, 96, 576, 192), (288, 384, 672, 480))

    def slot(s, c, other=0):
        return xall.at[pl.ds(base[other][s] + c * ROWS, ROWS), :]

    def x1(c):
        return rdma(slot(0, c), slot(1, c), x1_send.at[c], x1_recv.at[c], up)

    def x3(c):
        return rdma(slot(0, c), slot(3, c), x3_send.at[c], x3_recv.at[c], down)

    def x2(c):
        return rdma(slot(1, c), slot(2, c), x2_send.at[c], x2_recv.at[c], up)

    def to_twin(s, c):
        i = s * CHUNKS + c
        return rdma(slot(s, c), slot(s, c, 1), d_send.at[i], d_recv.at[i], twin)

    for c in range(CHUNKS):
        x1(c).start()
        x3(c).start()
    for c in range(CHUNKS):
        to_twin(0, c).start()

    def t_parts(kv, i):
        s = lax.rem(sg * (i - lev) + 8, 4)
        m = s - 4 * (s // 3)
        zt = lax.rem(half * HALF + i - sg * m + LEVELS, LEVELS)
        last = s // 2 - s // 3
        row = last * (576 + TOK * foreign) + (1 - last) * (288 * foreign + TOK * (s - s // 3))
        row = pl.multiple_of(row, TOK)
        idx = kv * 8 + foreign * 4 + s
        self_ = jnp.logical_and(zt == z, native)
        return goal_ref.at[kv, pl.ds(i * TOK, TOK), :], tg.at[kv, pl.ds(row, TOK), :], idx, zt, self_

    def send_targets(kv):
        for i in range(8):
            src, dst, idx, zt, self_ = t_parts(kv, i)

            @pl.when(self_)
            def _():
                pltpu.make_async_copy(src, dst, t_recv.at[idx]).start()

            @pl.when(jnp.logical_not(self_))
            def _():
                rdma(src, dst, t_send.at[kv * 8 + i], t_recv.at[idx], at_z(zt, kt)).start()

    send_targets(0)

    for i in range(4):
        wd = wg.at[:, i // 2, x, y, pl.ds((i % 2) * 64, 64), :]
        rdma(wsh, wd, w_send.at[0], w_recv.at[i], twin).wait_recv()

    def ag1(b, j):
        r = wg.at[b, :, x, y]
        return rdma(r, r, ag1_send.at[b * 3 + j], ag1_recv.at[b * 3 + j], (xpeer if b == 0 else ypeer)[j])

    def ag2(b, j):
        r = wg.at[0, :, :, y] if b == 0 else wg.at[1, :, x]
        return rdma(r, r, ag2_send.at[b * 3 + j], ag2_recv.at[b * 3 + j], (ypeer if b == 0 else xpeer)[j])

    pairs = [(b, j) for j in range(3) for b in range(2)]
    for b, j in pairs:
        ag1(b, j).start()
    for b, j in pairs:
        ag1(b, j).wait_recv()
    for b, j in pairs:
        ag2(b, j).start()

    for c in range(CHUNKS):
        x1(c).wait_recv()
        x2(c).start()
        to_twin(1, c).start()
        x3(c).wait_recv()
        to_twin(3, c).start()

    for b, j in pairs:
        ag2(b, j).wait_recv()
    for s in (0, 1, 3):
        for c in range(CHUNKS):
            to_twin(s, c).wait_recv()

    def forward(first, rows):
        w = jnp.concatenate([wg[0].reshape(D, 128), wg[1].reshape(D, 128)], axis=1)
        p = jnp.dot(xall[pl.ds(first, rows), :], w, preferred_element_type=f32)
        for kv in range(2):
            pred[kv, pl.ds(first, rows), :] = p[:, kv * 128:(kv + 1) * 128]

    def early(i, _):
        forward(pl.multiple_of(i * 288, 32), 288)
        return 0

    lax.fori_loop(0, 2, early, 0)
    for c in range(CHUNKS):
        x2(c).wait_recv()
        to_twin(2, c).start()
    send_targets(1)
    for c in range(CHUNKS):
        to_twin(2, c).wait_recv()
    forward(576, 192)

    first = (x, y)
    second = (y, x)
    peer1 = (xpeer, ypeer)
    peer2 = (ypeer, xpeer)

    def sem1(kv, ab, j):
        return (kv * 2 + ab) * 3 + j

    def g1(kv, ab, j):
        i = sem1(kv, ab, j)
        return rdma(gb.at[kv, ab, j], r1.at[kv, ab, j], g1_send.at[i], g1_recv.at[i], peer1[ab][j])

    def backward(kv):
        for i in range(8):
            dst = tg.at[kv, pl.ds(i * TOK, TOK), :]
            rdma(dst, dst, t_send.at[0], t_recv.at[kv * 8 + i], twin).wait_recv()
        et[kv] = jnp.transpose(pred[kv] - tg[kv].astype(f32)).astype(bf16)
        for j in range(4):
            for ab in range(2):
                t = lax.rem(first[ab] + j + 1, 4)
                if ab == 0:
                    block = xall[:, pl.ds(pl.multiple_of(t * 512, 512), 512)]
                else:
                    block = jnp.concatenate(
                        [xall[:, pl.ds(pl.multiple_of(2048 + i * 512 + t * 128, 128), 128)] for i in range(4)], axis=1
                    )
                g = jnp.dot(et[kv], block, preferred_element_type=f32)
                for i in range(4):
                    piece = g[:, i * 128:(i + 1) * 128]
                    if j < 3:
                        gb[kv, ab, j, i] = encode(piece)
                    else:
                        own[kv, ab, i] = piece
                if j < 3:
                    g1(kv, ab, j).start()

    def g2(kv, ab, j):
        i = sem1(kv, ab, j)
        return rdma(a1.at[kv, ab, j], r2.at[kv, ab, j], g2_send.at[i], g2_recv.at[i], peer2[ab][j])

    def sum1(kv):
        for ab in range(2):
            for j in range(3):
                g1(kv, ab, j).wait_recv()
        for j in range(4):
            for ab in range(2):
                i = lax.rem(second[ab] + j + 1, 4)
                v = own[kv, ab, i]
                for n in range(3):
                    v = v + decode(r1[kv, ab, n, i])
                if j < 3:
                    a1[kv, ab, j] = encode(v)
                    g2(kv, ab, j).start()
                else:
                    mid[kv, ab] = v

    m_own = z // CLASSES

    def g3_parts(kv, i):
        h2, c2 = i // 2, i % 2
        src = g3.at[kv, h2, pl.ds(c2 * 64, 64), :]
        self_ = jnp.logical_and(native, jnp.logical_and(half == h2, core == c2))
        return src, r3.at[kv, m_own], kv * 4 + m_own, at(h2, x, y, c2, col), self_

    def sum2(kv):
        for ab in range(2):
            for j in range(3):
                g2(kv, ab, j).wait_recv()
            v = mid[kv, ab]
            for n in range(3):
                v = v + decode(r2[kv, ab, n])
            g3[kv, ab] = encode(jnp.transpose(v))
            for i in (2 * ab, 2 * ab + 1):
                src, dst, idx, dev, self_ = g3_parts(kv, i)

                @pl.when(self_)
                def _():
                    pltpu.make_async_copy(src, dst, g3_recv.at[idx]).start()

                @pl.when(jnp.logical_not(self_))
                def _():
                    rdma(src, dst, g3_send.at[kv * 4 + i], g3_recv.at[idx], dev).start()

    def finish(kv):
        for i in range(4):
            rdma(r3.at[kv, i], r3.at[kv, i], g3_send.at[0], g3_recv.at[kv * 4 + i], twin).wait_recv()
        out_ref[kv] = (decode(r3[kv, 0]) + decode(r3[kv, 1])) + (decode(r3[kv, 2]) + decode(r3[kv, 3]))

    backward(0)
    backward(1)
    sum1(0)
    sum2(0)
    sum1(1)
    finish(0)
    sum2(1)
    finish(1)

    for m in range(4):
        @pl.when(jnp.logical_not(jnp.logical_and(cls + CLASSES * m == z, native)))
        def _():
            w_copy(m).wait_send()
    for c in range(CHUNKS):
        x1(c).wait_send()
        x2(c).wait_send()
        x3(c).wait_send()
        for s in range(4):
            to_twin(s, c).wait_send()
    for b, j in pairs:
        ag1(b, j).wait_send()
        ag2(b, j).wait_send()
    for kv in range(2):
        for i in range(8):
            src, dst, idx, zt, self_ = t_parts(kv, i)

            @pl.when(jnp.logical_not(self_))
            def _():
                rdma(src, dst, t_send.at[kv * 8 + i], t_recv.at[idx], at_z(zt, kt)).wait_send()
        for ab in range(2):
            for j in range(3):
                g1(kv, ab, j).wait_send()
                g2(kv, ab, j).wait_send()
        for i in range(4):
            src, dst, idx, dev, self_ = g3_parts(kv, i)

            @pl.when(jnp.logical_not(self_))
            def _():
                rdma(src, dst, g3_send.at[kv * 4 + i], g3_recv.at[idx], dev).wait_send()


def body(tokens, norm_gain, target, master, momentum):
    goal = jnp.transpose(target, (1, 0, 2))
    hbm = pl.BlockSpec(memory_space=pltpu.HBM)
    dma = pltpu.SemaphoreType.DMA
    V = pltpu.VMEM
    scratch = [
        V((TOK, D), bf16),
        V((1, D), f32),
        V((2, 64, 128), f32),
        V((768, D), bf16),
        V((2, 64, 128), bf16),
        V((2, 2, NX, NY, 128, 128), bf16),
        V((2, 768, 128), bf16),
        V((2, 768, 128), f32),
        V((2, 128, 768), bf16),
        V((2, 2, 4, 128, 128), f32),
        V((2, 2, 3, 4, 128, 128), bf16),
        V((2, 2, 3, 4, 128, 128), bf16),
        V((2, 2, 128, 128), f32),
        V((2, 2, 3, 128, 128), bf16),
        V((2, 2, 3, 128, 128), bf16),
        V((2, 2, 128, 128), bf16),
        V((2, 4, 64, 128), bf16),
        dma((3,)), dma((4,)), dma((4,)), dma((6,)), dma((6,)), dma((6,)), dma((6,)),
        dma((CHUNKS,)), dma((CHUNKS,)), dma((CHUNKS,)), dma((CHUNKS,)), dma((CHUNKS,)), dma((CHUNKS,)),
        dma((4 * CHUNKS,)), dma((4 * CHUNKS,)),
        dma((16,)), dma((16,)), dma((12,)), dma((12,)), dma((12,)), dma((12,)), dma((8,)), dma((8,)),
    ]
    summed = pl.pallas_call(
        kernel,
        out_shape=jax.ShapeDtypeStruct(master.shape, f32),
        in_specs=[hbm] * 4,
        out_specs=pl.BlockSpec(memory_space=pltpu.VMEM),
        scratch_shapes=scratch,
        compiler_params=pltpu.CompilerParams(
            collective_id=0, has_side_effects=True, vmem_limit_bytes=63 * 1024 * 1024
        ),
        cost_estimate=pl.CostEstimate(flops=3_300_000_000, bytes_accessed=2_000_000, transcendentals=0),
    )(tokens, norm_gain.reshape(1, D), goal, master)
    delta = summed * (inner_rate / 64)
    new_momentum = decay_rate * momentum + delta
    new_master = master - outer_rate * (delta + decay_rate * new_momentum)
    return (new_master, new_momentum)


def solution(mesh):
    in_specs = (
        P(("rep", "fsdp"), None),
        P(),
        P("rep", None, "fsdp"),
        P(None, "rep", "fsdp"),
        P(None, "rep", "fsdp"),
    )
    out_specs = (P(None, "rep", "fsdp"), P(None, "rep", "fsdp"))
    return jax.shard_map(body, mesh=mesh, in_specs=in_specs, out_specs=out_specs, check_vma=False)
```

time: 106 us -> 103 us (0.972)
  local copies, waits for them, and re-layouts: 4.9 us -> 1.8 us
  Pallas kernels: 101 us -> 98.5 us
  other arithmetic: 0 us -> 1.51 us
    unnamed x11 -> x5, local copies, waits for them, and re-layouts: 4.9 us -> 1.8 us
    pallas_call x1, Pallas kernels: 101 us -> 98.5 us  [body(): pl.pallas_call(kernel, out_shape=jax.ShapeDtypeStruct(master.shape, f32),...]
    sub x0 -> x1, other arithmetic: none -> 1.51 us  [body(): new_master = master - outer_rate * (delta + decay_rate * new_momentum)]
where the time goes in v2:
time: 103 us; the launch traced here: 102 us
  Pallas kernels  98.5 us (96%)
  local copies, waits for them, and re-layouts  1.8 us (2%)
  other arithmetic  1.51 us (1%)
    pallas_call x1, Pallas kernels, body(): pl.pallas_call(kernel, out_shape=jax.ShapeDtypeStruct(master.shape, f32),...  98.5 us

profile of v2, /device:TPU:1, one launch (start us, length us, event | category | flops | bytes accessed | tf_op | source)
XLA Modules:
  0.0 102.4 jit_solution(7965429573394609584)
XLA Ops:
  0.6 1.8 %copy.9 = bf16[768,2,128]{2,0,1:T(8,128)(2,1)} copy(bf16[768,2,128]{2,1,0:T(2,128)(2,1)} %param.7) | data formatting | bytes 786432 | tf_op args[2]
  2.4 0.0 copy-start
  2.4 0.0 copy-start.1
  2.4 98.5 %shard_map.68 = f32[2,64,128]{2,1,0:T(8,128)} custom-call(bf16[96,4096]{1,0:T(8,128)(2,1)} %tok_ref.1, f32[1,4096]{1,0:T(1,128)} %bitcast.5, bf16[2,768,128]{2,1,0:T(8,128)(2,1)} %bitcast.4, f32[2,64,128]{2,1,0:T(8,128)} %master_ref.1), custom_call_target="tpu_custom_call" | custom-call | flops 3300000000 | bytes 2000000 | tf_op jit(solution)/shard_map/pallas_call | solution.py:390
  100.9 0.0 copy-done
  100.9 0.0 copy-done.1
  100.9 1.5 %multiply_subtract_fusion = (f32[2,64,128]{2,1,0:T(8,128)}, f32[2,64,128]{2,1,0:T(8,128)}) fusion(f32[2,64,128]{2,1,0:T(8,128)S(1)} %copy-done, f32[2,64,128]{2,1,0:T(8,128)} %shard_map.68, f32[2,64,128]{2,1,0:T(8,128)S(1)} %copy-done.1), kind=kLoop, calls=%fused_computation.1 | loop fusion | flops 114688 | bytes 327680 | tf_op jit(solution)/shard_map/sub | solution.py:403
Async XLA Ops:
  2.4 98.5 %copy-start = (f32[2,64,128]{2,1,0:T(8,128)S(1)}, f32[2,64,128]{2,1,0:T(8,128)}, u32[]{:S(2)}) copy-start(f32[2,64,128]{2,1,0:T(8,128)} %master_ref.1) | copy-start | bytes 196612
  2.4 98.5 %copy-start.1 = (f32[2,64,128]{2,1,0:T(8,128)S(1)}, f32[2,64,128]{2,1,0:T(8,128)}, u32[]{:S(2)}) copy-start(f32[2,64,128]{2,1,0:T(8,128)} %param.9) | copy-start | bytes 196612

commit v3 on v2

--- a/solution.py
+++ b/solution.py
@@ -35,16 +35,16 @@
 
 
 def kernel(
-    tok_ref, gain_ref, goal_ref, master_ref,
+    tok_ref, gain_ref, tgt_ref, master_ref,
     out_ref,
-    xin, gain, mst, xall, wsh, wg, tg, pred, et, own, gb, r1, mid, a1, r2, g3, r3,
+    xin, gain, mst, tin, goal, raw, xall, wsh, wg, tg, pred, et, own, gb, r1, mid, a1, r2, g3, r3,
     in_sem, w_send, w_recv, ag1_send, ag1_recv, ag2_send, ag2_recv,
     x1_send, x1_recv, x3_send, x3_recv, x2_send, x2_recv, d_send, d_recv,
     t_send, t_recv, g1_send, g1_recv, g2_send, g2_recv, g3_send, g3_recv,
 ):
     loads = [
         pltpu.make_async_copy(src, dst, in_sem.at[i])
-        for i, (src, dst) in enumerate(((tok_ref, xin), (gain_ref, gain), (master_ref, mst)))
+        for i, (src, dst) in enumerate(((master_ref, mst), (tok_ref, xin), (gain_ref, gain), (tgt_ref, tin)))
     ]
     for load in loads:
         load.start()
@@ -102,13 +102,8 @@
         def _():
             hello(at(h2, x, y, c2, col))
 
-    for load in loads:
-        load.wait()
+    loads[0].wait()
     wsh[...] = mst[...].astype(bf16)
-    for c in range(CHUNKS):
-        v = xin[pl.ds(c * ROWS, ROWS), :].astype(f32)
-        scale = lax.rsqrt(jnp.mean(v * v, axis=-1, keepdims=True) + norm_eps)
-        xall[pl.ds(c * ROWS, ROWS), :] = (v * scale * gain[...]).astype(bf16)
 
     pl.semaphore_wait(barrier, 9 + 8 - 2 * (1 - foreign))
 
@@ -135,10 +130,10 @@
         return xall.at[pl.ds(base[other][s] + c * ROWS, ROWS), :]
 
     def x1(c):
-        return rdma(slot(0, c), slot(1, c), x1_send.at[c], x1_recv.at[c], up)
+        return rdma(tok_ref.at[pl.ds(c * ROWS, ROWS), :], raw.at[0, c], x1_send.at[c], x1_recv.at[c], up)
 
     def x3(c):
-        return rdma(slot(0, c), slot(3, c), x3_send.at[c], x3_recv.at[c], down)
+        return rdma(tok_ref.at[pl.ds(c * ROWS, ROWS), :], raw.at[1, c], x3_send.at[c], x3_recv.at[c], down)
 
     def x2(c):
         return rdma(slot(1, c), slot(2, c), x2_send.at[c], x2_recv.at[c], up)
@@ -147,11 +142,24 @@
         i = s * CHUNKS + c
         return rdma(slot(s, c), slot(s, c, 1), d_send.at[i], d_recv.at[i], twin)
 
+    def norm(v, s, c):
+        v = v.astype(f32)
+        scale = lax.rsqrt(jnp.mean(v * v, axis=-1, keepdims=True) + norm_eps)
+        slot(s, c)[...] = (v * scale * gain[...]).astype(bf16)
+
     for c in range(CHUNKS):
         x1(c).start()
+    for c in range(CHUNKS):
         x3(c).start()
-    for c in range(CHUNKS):
+    loads[1].wait()
+    loads[2].wait()
+    for c in range(CHUNKS):
+        norm(xin[pl.ds(c * ROWS, ROWS), :], 0, c)
         to_twin(0, c).start()
+    loads[3].wait()
+    for i in range(8):
+        rows = pl.ds(i * TOK, TOK)
+        goal[:, rows, :] = jnp.swapaxes(tin[rows], 0, 1)
 
     def t_parts(kv, i):
         s = lax.rem(sg * (i - lev) + 8, 4)
@@ -162,7 +170,7 @@
         row = pl.multiple_of(row, TOK)
         idx = kv * 8 + foreign * 4 + s
         self_ = jnp.logical_and(zt == z, native)
-        return goal_ref.at[kv, pl.ds(i * TOK, TOK), :], tg.at[kv, pl.ds(row, TOK), :], idx, zt, self_
+        return goal.at[kv, pl.ds(i * TOK, TOK), :], tg.at[kv, pl.ds(row, TOK), :], idx, zt, self_
 
     def send_targets(kv):
         for i in range(8):
@@ -200,9 +208,12 @@
 
     for c in range(CHUNKS):
         x1(c).wait_recv()
+        norm(raw[0, c], 1, c)
         x2(c).start()
         to_twin(1, c).start()
+    for c in range(CHUNKS):
         x3(c).wait_recv()
+        norm(raw[1, c], 3, c)
         to_twin(3, c).start()
 
     for b, j in pairs:
@@ -235,54 +246,41 @@
     peer1 = (xpeer, ypeer)
     peer2 = (ypeer, xpeer)
 
-    def sem1(kv, ab, j):
-        return (kv * 2 + ab) * 3 + j
-
-    def g1(kv, ab, j):
-        i = sem1(kv, ab, j)
-        return rdma(gb.at[kv, ab, j], r1.at[kv, ab, j], g1_send.at[i], g1_recv.at[i], peer1[ab][j])
+    def g1(kv, ab, n, j):
+        i = ((kv * 2 + ab) * 4 + n) * 3 + j
+        return rdma(gb.at[kv, ab, n, j], r1.at[kv, ab, n, j], g1_send.at[i], g1_recv.at[i], peer1[ab][j])
 
     def backward(kv):
         for i in range(8):
             dst = tg.at[kv, pl.ds(i * TOK, TOK), :]
             rdma(dst, dst, t_send.at[0], t_recv.at[kv * 8 + i], twin).wait_recv()
         et[kv] = jnp.transpose(pred[kv] - tg[kv].astype(f32)).astype(bf16)
-        for j in range(4):
+        for n in range(4):
             for ab in range(2):
-                t = lax.rem(first[ab] + j + 1, 4)
-                if ab == 0:
-                    block = xall[:, pl.ds(pl.multiple_of(t * 512, 512), 512)]
-                else:
-                    block = jnp.concatenate(
-                        [xall[:, pl.ds(pl.multiple_of(2048 + i * 512 + t * 128, 128), 128)] for i in range(4)], axis=1
-                    )
+                i = lax.rem(second[ab] + n + 1, 4)
+                ts = [lax.rem(first[ab] + j + 1, 4) for j in range(4)]
+                starts = [(t * 512 + i * 128) if ab == 0 else (2048 + i * 512 + t * 128) for t in ts]
+                block = jnp.concatenate([xall[:, pl.ds(pl.multiple_of(c0, 128), 128)] for c0 in starts], axis=1)
                 g = jnp.dot(et[kv], block, preferred_element_type=f32)
-                for i in range(4):
-                    piece = g[:, i * 128:(i + 1) * 128]
-                    if j < 3:
-                        gb[kv, ab, j, i] = encode(piece)
-                    else:
-                        own[kv, ab, i] = piece
-                if j < 3:
-                    g1(kv, ab, j).start()
+                for j in range(3):
+                    gb[kv, ab, n, j] = encode(g[:, j * 128:(j + 1) * 128])
+                    g1(kv, ab, n, j).start()
+                own[kv, ab, n] = g[:, 384:]
 
     def g2(kv, ab, j):
-        i = sem1(kv, ab, j)
+        i = (kv * 2 + ab) * 3 + j
         return rdma(a1.at[kv, ab, j], r2.at[kv, ab, j], g2_send.at[i], g2_recv.at[i], peer2[ab][j])
 
     def sum1(kv):
-        for ab in range(2):
-            for j in range(3):
-                g1(kv, ab, j).wait_recv()
-        for j in range(4):
+        for n in range(4):
             for ab in range(2):
-                i = lax.rem(second[ab] + j + 1, 4)
-                v = own[kv, ab, i]
-                for n in range(3):
-                    v = v + decode(r1[kv, ab, n, i])
-                if j < 3:
-                    a1[kv, ab, j] = encode(v)
-                    g2(kv, ab, j).start()
+                v = own[kv, ab, n]
+                for j in range(3):
+                    g1(kv, ab, n, j).wait_recv()
+                    v = v + decode(r1[kv, ab, n, j])
+                if n < 3:
+                    a1[kv, ab, n] = encode(v)
+                    g2(kv, ab, n).start()
                 else:
                     mid[kv, ab] = v
 
@@ -321,10 +319,10 @@
     backward(0)
     backward(1)
     sum1(0)
+    sum1(1)
     sum2(0)
-    sum1(1)
+    sum2(1)
     finish(0)
-    sum2(1)
     finish(1)
 
     for m in range(4):
@@ -349,8 +347,9 @@
                 rdma(src, dst, t_send.at[kv * 8 + i], t_recv.at[idx], at_z(zt, kt)).wait_send()
         for ab in range(2):
             for j in range(3):
-                g1(kv, ab, j).wait_send()
                 g2(kv, ab, j).wait_send()
+                for n in range(4):
+                    g1(kv, ab, n, j).wait_send()
         for i in range(4):
             src, dst, idx, dev, self_ = g3_parts(kv, i)
 
@@ -360,7 +359,6 @@
 
 
 def body(tokens, norm_gain, target, master, momentum):
-    goal = jnp.transpose(target, (1, 0, 2))
     hbm = pl.BlockSpec(memory_space=pltpu.HBM)
     dma = pltpu.SemaphoreType.DMA
     V = pltpu.VMEM
@@ -368,6 +366,9 @@
         V((TOK, D), bf16),
         V((1, D), f32),
         V((2, 64, 128), f32),
+        V((768, 2, 128), bf16),
+        V((2, 768, 128), bf16),
+        V((2, CHUNKS, ROWS, D), bf16),
         V((768, D), bf16),
         V((2, 64, 128), bf16),
         V((2, 2, NX, NY, 128, 128), bf16),
@@ -375,17 +376,17 @@
         V((2, 768, 128), f32),
         V((2, 128, 768), bf16),
         V((2, 2, 4, 128, 128), f32),
-        V((2, 2, 3, 4, 128, 128), bf16),
-        V((2, 2, 3, 4, 128, 128), bf16),
+        V((2, 2, 4, 3, 128, 128), bf16),
+        V((2, 2, 4, 3, 128, 128), bf16),
         V((2, 2, 128, 128), f32),
         V((2, 2, 3, 128, 128), bf16),
         V((2, 2, 3, 128, 128), bf16),
         V((2, 2, 128, 128), bf16),
         V((2, 4, 64, 128), bf16),
-        dma((3,)), dma((4,)), dma((4,)), dma((6,)), dma((6,)), dma((6,)), dma((6,)),
+        dma((4,)), dma((4,)), dma((4,)), dma((6,)), dma((6,)), dma((6,)), dma((6,)),
         dma((CHUNKS,)), dma((CHUNKS,)), dma((CHUNKS,)), dma((CHUNKS,)), dma((CHUNKS,)), dma((CHUNKS,)),
         dma((4 * CHUNKS,)), dma((4 * CHUNKS,)),
-        dma((16,)), dma((16,)), dma((12,)), dma((12,)), dma((12,)), dma((12,)), dma((8,)), dma((8,)),
+        dma((16,)), dma((16,)), dma((48,)), dma((48,)), dma((12,)), dma((12,)), dma((8,)), dma((8,)),
     ]
     summed = pl.pallas_call(
         kernel,
@@ -394,10 +395,10 @@
         out_specs=pl.BlockSpec(memory_space=pltpu.VMEM),
         scratch_shapes=scratch,
         compiler_params=pltpu.CompilerParams(
-            collective_id=0, has_side_effects=True, vmem_limit_bytes=63 * 1024 * 1024
+            collective_id=0, has_side_effects=True, vmem_limit_bytes=60 * 1024 * 1024
         ),
         cost_estimate=pl.CostEstimate(flops=3_300_000_000, bytes_accessed=2_000_000, transcendentals=0),
-    )(tokens, norm_gain.reshape(1, D), goal, master)
+    )(tokens, norm_gain.reshape(1, D), target, master)
     delta = summed * (inner_rate / 64)
     new_momentum = decay_rate * momentum + delta
     new_master = master - outer_rate * (delta + decay_rate * new_momentum)

time: 103 us -> 95.6 us (0.928)
  Pallas kernels: 98.5 us -> 93.2 us
  local copies, waits for them, and re-layouts: 1.8 us -> 0.01 us
    pallas_call x1, Pallas kernels: 98.5 us -> 93.2 us  [body(): pl.pallas_call(kernel, out_shape=jax.ShapeDtypeStruct(master.shape, f32),...]
    unnamed x5 -> x4, local copies, waits for them, and re-layouts: 1.8 us -> 0.01 us
where the time goes in v3:
time: 95.6 us; the launch traced here: 95.4 us
  Pallas kernels  93.2 us (97%)
  other arithmetic  1.51 us (2%)
    pallas_call x1, Pallas kernels, body(): pl.pallas_call(kernel, out_shape=jax.ShapeDtypeStruct(master.shape, f32),...  93.2 us

profile of v3, /device:TPU:1, one launch (start us, length us, event | category | flops | bytes accessed | tf_op | source)
XLA Modules:
  0.0 95.4 jit_solution(15979487514481605720)
XLA Ops:
  0.6 0.0 copy-start
  0.6 0.0 copy-start.1
  0.7 93.2 %shard_map.68 = f32[2,64,128]{2,1,0:T(8,128)} custom-call(bf16[96,4096]{1,0:T(8,128)(2,1)} %tok_ref.1, f32[1,4096]{1,0:T(1,128)} %bitcast.1, bf16[768,2,128]{2,1,0:T(2,128)(2,1)} %tgt_ref.1, f32[2,64,128]{2,1,0:T(8,128)} %master_ref.1), custom_call_target="tpu_custom_call" | custom-call | flops 3300000000 | bytes 2000000 | tf_op jit(solution)/shard_map/pallas_call | solution.py:391
  93.9 0.0 copy-done
  93.9 0.0 copy-done.1
  93.9 1.5 %multiply_subtract_fusion = (f32[2,64,128]{2,1,0:T(8,128)}, f32[2,64,128]{2,1,0:T(8,128)}) fusion(f32[2,64,128]{2,1,0:T(8,128)S(1)} %copy-done, f32[2,64,128]{2,1,0:T(8,128)} %shard_map.68, f32[2,64,128]{2,1,0:T(8,128)S(1)} %copy-done.1), kind=kLoop, calls=%fused_computation | loop fusion | flops 114688 | bytes 327680 | tf_op jit(solution)/shard_map/sub | solution.py:404
Async XLA Ops:
  0.6 93.2 %copy-start = (f32[2,64,128]{2,1,0:T(8,128)S(1)}, f32[2,64,128]{2,1,0:T(8,128)}, u32[]{:S(2)}) copy-start(f32[2,64,128]{2,1,0:T(8,128)} %master_ref.1) | copy-start | bytes 196612
  0.6 93.2 %copy-start.1 = (f32[2,64,128]{2,1,0:T(8,128)S(1)}, f32[2,64,128]{2,1,0:T(8,128)}, u32[]{:S(2)}) copy-start(f32[2,64,128]{2,1,0:T(8,128)} %param.9) | copy-start | bytes 196612

commit v4 on v3

--- a/solution.py
+++ b/solution.py
@@ -16,8 +16,9 @@
 LEVELS = 16
 HALF = 8
 CLASSES = 4
+FAR_FIRST = (2, 1, 3, 4)
 TOK = 96
-CHUNKS = 3
+CHUNKS = 2
 ROWS = TOK // CHUNKS
 D = 4096
 f32 = jnp.float32
@@ -76,8 +77,8 @@
             src_ref=src, dst_ref=dst, send_sem=ss, recv_sem=rs, device_id=dev, device_id_type=MESH
         )
 
-    xpeer = [at(half, lax.rem(x + j, NX), y, core, lev) for j in (1, 2, 3)]
-    ypeer = [at(half, x, lax.rem(y + j, NY), core, lev) for j in (1, 2, 3)]
+    xpeer = [at(half, lax.rem(x + j, NX), y, core, lev) for j in FAR_FIRST[:3]]
+    ypeer = [at(half, x, lax.rem(y + j, NY), core, lev) for j in FAR_FIRST[:3]]
     up = at_z(z + fdir, core)
     down = at_z(z - fdir, core)
     twin = at_z(z, 1 - core)
@@ -257,8 +258,8 @@
         et[kv] = jnp.transpose(pred[kv] - tg[kv].astype(f32)).astype(bf16)
         for n in range(4):
             for ab in range(2):
-                i = lax.rem(second[ab] + n + 1, 4)
-                ts = [lax.rem(first[ab] + j + 1, 4) for j in range(4)]
+                i = lax.rem(second[ab] + FAR_FIRST[n], 4)
+                ts = [lax.rem(first[ab] + j, 4) for j in FAR_FIRST]
                 starts = [(t * 512 + i * 128) if ab == 0 else (2048 + i * 512 + t * 128) for t in ts]
                 block = jnp.concatenate([xall[:, pl.ds(pl.multiple_of(c0, 128), 128)] for c0 in starts], axis=1)
                 g = jnp.dot(et[kv], block, preferred_element_type=f32)

time: 95.6 us -> 95.2 us (level)
  no operation moved by 1% of the time
where the time goes in v4:
time: 95.2 us; the launch traced here: 95 us
  Pallas kernels  92.8 us (97%)
  other arithmetic  1.51 us (2%)
    pallas_call x1, Pallas kernels, body(): pl.pallas_call(kernel, out_shape=jax.ShapeDtypeStruct(master.shape, f32),...  92.8 us

profile of v4, /device:TPU:1, one launch (start us, length us, event | category | flops | bytes accessed | tf_op | source)
XLA Modules:
  0.0 95.0 jit_solution(8183876649292719801)
XLA Ops:
  0.6 0.0 copy-start
  0.6 0.0 copy-start.1
  0.7 92.8 %shard_map.68 = f32[2,64,128]{2,1,0:T(8,128)} custom-call(bf16[96,4096]{1,0:T(8,128)(2,1)} %tok_ref.1, f32[1,4096]{1,0:T(1,128)} %bitcast.1, bf16[768,2,128]{2,1,0:T(2,128)(2,1)} %tgt_ref.1, f32[2,64,128]{2,1,0:T(8,128)} %master_ref.1), custom_call_target="tpu_custom_call" | custom-call | flops 3300000000 | bytes 2000000 | tf_op jit(solution)/shard_map/pallas_call | solution.py:392
  93.5 0.0 copy-done
  93.5 0.0 copy-done.1
  93.5 1.5 %multiply_subtract_fusion = (f32[2,64,128]{2,1,0:T(8,128)}, f32[2,64,128]{2,1,0:T(8,128)}) fusion(f32[2,64,128]{2,1,0:T(8,128)S(1)} %copy-done, f32[2,64,128]{2,1,0:T(8,128)} %shard_map.68, f32[2,64,128]{2,1,0:T(8,128)S(1)} %copy-done.1), kind=kLoop, calls=%fused_computation | loop fusion | flops 114688 | bytes 327680 | tf_op jit(solution)/shard_map/sub | solution.py:405
Async XLA Ops:
  0.6 92.8 %copy-start = (f32[2,64,128]{2,1,0:T(8,128)S(1)}, f32[2,64,128]{2,1,0:T(8,128)}, u32[]{:S(2)}) copy-start(f32[2,64,128]{2,1,0:T(8,128)} %master_ref.1) | copy-start | bytes 196612
  0.6 92.8 %copy-start.1 = (f32[2,64,128]{2,1,0:T(8,128)S(1)}, f32[2,64,128]{2,1,0:T(8,128)}, u32[]{:S(2)}) copy-start(f32[2,64,128]{2,1,0:T(8,128)} %param.9) | copy-start | bytes 196612

commit v5 on v4

--- a/solution.py
+++ b/solution.py
@@ -174,7 +174,7 @@
         return goal.at[kv, pl.ds(i * TOK, TOK), :], tg.at[kv, pl.ds(row, TOK), :], idx, zt, self_
 
     def send_targets(kv):
-        for i in range(8):
+        for i in (0, 7, 1, 6, 2, 5, 3, 4):
             src, dst, idx, zt, self_ = t_parts(kv, i)
 
             @pl.when(self_)

time: 95.2 us -> 95.2 us (level)
  no operation moved by 1% of the time
where the time goes in v5:
time: 95.2 us; the launch traced here: 95 us
  Pallas kernels  92.8 us (97%)
  other arithmetic  1.51 us (2%)
    pallas_call x1, Pallas kernels, body(): pl.pallas_call(kernel, out_shape=jax.ShapeDtypeStruct(master.shape, f32),...  92.8 us

profile of v5, /device:TPU:1, one launch (start us, length us, event | category | flops | bytes accessed | tf_op | source)
XLA Modules:
  0.0 95.0 jit_solution(4474272304106125601)
XLA Ops:
  0.6 0.0 copy-start
  0.6 0.0 copy-start.1
  0.7 92.8 %shard_map.68 = f32[2,64,128]{2,1,0:T(8,128)} custom-call(bf16[96,4096]{1,0:T(8,128)(2,1)} %tok_ref.1, f32[1,4096]{1,0:T(1,128)} %bitcast.1, bf16[768,2,128]{2,1,0:T(2,128)(2,1)} %tgt_ref.1, f32[2,64,128]{2,1,0:T(8,128)} %master_ref.1), custom_call_target="tpu_custom_call" | custom-call | flops 3300000000 | bytes 2000000 | tf_op jit(solution)/shard_map/pallas_call | solution.py:392
  93.4 0.0 copy-done
  93.5 0.0 copy-done.1
  93.5 1.5 %multiply_subtract_fusion = (f32[2,64,128]{2,1,0:T(8,128)}, f32[2,64,128]{2,1,0:T(8,128)}) fusion(f32[2,64,128]{2,1,0:T(8,128)S(1)} %copy-done, f32[2,64,128]{2,1,0:T(8,128)} %shard_map.68, f32[2,64,128]{2,1,0:T(8,128)S(1)} %copy-done.1), kind=kLoop, calls=%fused_computation | loop fusion | flops 114688 | bytes 327680 | tf_op jit(solution)/shard_map/sub | solution.py:405
Async XLA Ops:
  0.6 92.8 %copy-start = (f32[2,64,128]{2,1,0:T(8,128)S(1)}, f32[2,64,128]{2,1,0:T(8,128)}, u32[]{:S(2)}) copy-start(f32[2,64,128]{2,1,0:T(8,128)} %master_ref.1) | copy-start | bytes 196612
  0.6 92.8 %copy-start.1 = (f32[2,64,128]{2,1,0:T(8,128)S(1)}, f32[2,64,128]{2,1,0:T(8,128)}, u32[]{:S(2)}) copy-start(f32[2,64,128]{2,1,0:T(8,128)} %param.9) | copy-start | bytes 196612
